TPU v7x, 128 devices: a whole 4x4x4 slice. The times are simulated.
128 devices in a mesh: gr: 8 (over y_hi, z), gc: 16 (over y_lo, x, core).
Axes of the slice: x: 4, y: 4 (y_hi: 2, y_lo: 2; y = y_hi * 2 + y_lo), z: 4, core: 2. Of those that a mesh axis runs over, the one named last changes fastest.
Arguments:
- student: bfloat16 [16384, 1024], P(('gr', 'gc')), may hold values from -500 to 500
- teacher: bfloat16 [16384, 1024], P(('gr', 'gc')), may hold values from -500 to 500
Outputs:
- student_grad: float32 [16384, 1024], P(('gr', 'gc'))
All inputs are finite; a program needn't handle non-finite values.
Results may differ from a plain program's by a relative error of at most 0.0085.
Values may be sent and summed in bfloat16 or wider, within the bound.
A program may use at most 64 MiB of HBM per device.

v0:
```python
import jax
import jax.numpy as jnp
from jax import lax
from jax.sharding import PartitionSpec as P

D = 1024


def unit_rows(embedded):
    values = embedded.astype(jnp.float32)
    inverse_rms = lax.rsqrt(jnp.mean(values * values, axis=-1, keepdims=True) + 1e-06)
    unit = (values * inverse_rms * D ** (-0.5)).astype(jnp.bfloat16)
    return (unit, inverse_rms)


def mismatch_of(piece_s, piece_t, other_s, other_t):
    sim_student = lax.dot_general(
        piece_s, other_s, (((1,), (1,)), ((), ())), preferred_element_type=jnp.float32
    )
    sim_teacher = lax.dot_general(
        piece_t, other_t, (((1,), (1,)), ((), ())), preferred_element_type=jnp.float32
    )
    stretch = 0.5 * D**0.5
    return jnp.tanh(stretch * (sim_student - sim_teacher)).astype(jnp.bfloat16)


def local(student, teacher):
    unit_s, inv_s = unit_rows(student)
    unit_t, inv_t = unit_rows(teacher)
    column_s, column_t = (
        lax.all_gather(unit_s, "gr", axis=0, tiled=True),
        lax.all_gather(unit_t, "gr", axis=0, tiled=True),
    )
    row_s, row_t = (
        lax.all_gather(unit_s, "gc", axis=0, tiled=True),
        lax.all_gather(unit_t, "gc", axis=0, tiled=True),
    )
    mismatch = mismatch_of(row_s, row_t, column_s, column_t)
    pull = lax.psum_scatter(
        jnp.dot(mismatch, column_s, preferred_element_type=jnp.float32),
        "gc",
        scatter_dimension=0,
        tiled=True,
    )
    unit_float = unit_s.astype(jnp.float32)
    radial = jnp.sum(unit_float * pull, axis=-1, keepdims=True)
    total_rows = unit_s.shape[0] * lax.axis_size("gr") * lax.axis_size("gc")
    factor = 12.0 * (D / total_rows) ** 0.5
    return factor * inv_s * (pull - radial * unit_float)


def solution(mesh):
    in_specs = (P(("gr", "gc"), None), P(("gr", "gc"), None))
    out_specs = P(("gr", "gc"), None)
    return jax.shard_map(local, mesh=mesh, in_specs=in_specs, out_specs=out_specs, check_vma=False)
```

profile of v0, /device:TPU:0, one launch (start us, length us, event | category | flops | bytes accessed | tf_op | source)
XLA Modules:
  0.0 295.6 jit_solution(11600875809418182227)
XLA Ops:
  6.5 0.0 all-gather.7.cloned.1.call-start
  6.5 1.1 fusion.4
  7.6 1.8 fusion.6
  9.4 0.0 all-gather.7.cloned.1.call-update
  9.4 0.0 all-gather.5.cloned.1.call-start
  9.5 0.7 all-gather.5.cloned.1.call-update
  10.2 0.0 all-gather.11.cloned.1.call-start
  10.2 1.1 fusion.7
  11.3 1.8 fusion.9
  13.1 0.0 all-gather.11.cloned.1.call-update
  13.2 0.0 all-gather.9.cloned.1.call-start
  13.2 0.5 all-gather.9.cloned.1.call-update
  13.7 0.0 reduce-scatter.2.cloned.1.call-start
  13.8 52.6 %all-gather.7.cloned.1.call-done = bf16[1024,1024]{1,0:T(8,128)(2,1)} async-done(((bf16[128,1024]{1,0:T(8,128)(2,1)}), bf16[1024,1024]{1,0:T(8,128)(2,1)}) %all-gather.7.cloned.1.call-update) | async-done | bytes 2097168 | tf_op jit(solution)/shard_map/all_gather | solution.py:31
  66.4 0.0 copy-start.1
  66.4 36.8 %all-gather.5.cloned.1.call-done = bf16[2048,1024]{1,0:T(8,128)(2,1)} async-done(((bf16[128,1024]{1,0:T(8,128)(2,1)}), bf16[2048,1024]{1,0:T(8,128)(2,1)}) %all-gather.5.cloned.1.call-update) | async-done | bytes 4194320 | tf_op jit(solution)/shard_map/all_gather | solution.py:35
  103.2 10.7 %fusion.14 = f32[2048,1024]{1,0:T(8,128)} fusion(bf16[2048,1024]{1,0:T(8,128)(2,1)} %all-gather.5.cloned.1.call-done, bf16[1024,1024]{1,0:T(8,128)(2,1)} %all-gather.7.cloned.1.call-done), kind=kOutput, calls=%fused_computation.23 | convolution fusion | flops 4294967296 | bytes 14680064 | tf_op jit(solution)/shard_map/dot_general | solution.py:17
  113.8 46.0 %all-gather.11.cloned.1.call-done = bf16[1024,1024]{1,0:T(8,128)(2,1)} async-done(((bf16[128,1024]{1,0:T(8,128)(2,1)}), bf16[1024,1024]{1,0:T(8,128)(2,1)}) %all-gather.11.cloned.1.call-update) | async-done | bytes 2097168 | tf_op jit(solution)/shard_map/all_gather | solution.py:32
  159.8 36.6 %all-gather.9.cloned.1.call-done = bf16[2048,1024]{1,0:T(8,128)(2,1)} async-done(((bf16[128,1024]{1,0:T(8,128)(2,1)}), bf16[2048,1024]{1,0:T(8,128)(2,1)}) %all-gather.9.cloned.1.call-update) | async-done | bytes 4194320 | tf_op jit(solution)/shard_map/all_gather | solution.py:36
  196.4 0.0 copy-done.1
  196.4 14.5 %fusion = f32[2048,1024]{1,0:T(8,128)} fusion(bf16[1024,1024]{1,0:T(8,128)(2,1)S(1)} %copy-done.1, f32[2048,1024]{1,0:T(8,128)} %fusion.14, bf16[2048,1024]{1,0:T(8,128)(2,1)} %all-gather.9.cloned.1.call-done, bf16[1024,1024]{1,0:T(8,128)(2,1)} %all-gather.11.cloned.1.call-done), kind=kOutput, calls=%fused_computation.1 | convolution fusion | flops 8596226048 | bytes 25165824 | tf_op jit(solution)/shard_map/dot_general | solution.py:40
  210.9 0.0 copy-start
  210.9 0.0 reduce-scatter.2.cloned.1.call-update
  211.0 74.8 %reduce-scatter.2.cloned.1.call-done = f32[128,1024]{1,0:T(8,128)} async-done(((f32[2048,1024]{1,0:T(8,128)}), f32[128,1024]{1,0:T(8,128)}) %reduce-scatter.2.cloned.1.call-update) | async-done | bytes 524304 | tf_op jit(solution)/shard_map/reduce_scatter | solution.py:39
  285.8 0.0 copy-done
  285.8 1.3 fusion.10
  287.0 2.1 fusion.12
  (2 shorter events, 0.0 us)
Async XLA Ops:
  6.5 59.8 %all-gather.7.cloned.1.call-start = ((), (), s32[]{:S(2)}) async-start(), calls=%async_computation.2 | async-start | bytes 2359296 | tf_op jit(solution)/shard_map/all_gather | solution.py:31
  9.4 93.7 %all-gather.5.cloned.1.call-start = ((), (), s32[]{:S(2)}) async-start(), calls=%async_computation.1 | async-start | bytes 4456448 | tf_op jit(solution)/shard_map/all_gather | solution.py:35
  10.2 149.6 %all-gather.11.cloned.1.call-start = ((), (), s32[]{:S(2)}) async-start(), calls=%async_computation.4 | async-start | bytes 2359296 | tf_op jit(solution)/shard_map/all_gather | solution.py:32
  13.2 183.2 %all-gather.9.cloned.1.call-start = ((), (), s32[]{:S(2)}) async-start(), calls=%async_computation.3 | async-start | bytes 4456448 | tf_op jit(solution)/shard_map/all_gather | solution.py:36
  13.7 272.0 %reduce-scatter.2.cloned.1.call-start = ((), (), s32[]{:S(2)}) async-start(), calls=%async_computation.5 | async-start | bytes 8912896 | tf_op jit(solution)/shard_map/reduce_scatter | solution.py:39
  66.4 130.0 %copy-start.1 = (bf16[1024,1024]{1,0:T(8,128)(2,1)S(1)}, bf16[1024,1024]{1,0:T(8,128)(2,1)}, u32[]{:S(2)}) copy-start(bf16[1024,1024]{1,0:T(8,128)(2,1)} %all-gather.7.cloned.1.call-done) | copy-start | bytes 6291460
  210.9 74.8 %copy-start = (bf16[128,1024]{1,0:T(8,128)(2,1)S(1)}, bf16[128,1024]{1,0:T(8,128)(2,1)}, u32[]{:S(2)}) copy-start(bf16[128,1024]{1,0:T(8,128)(2,1)} %param.2) | copy-start | bytes 786436
Sparse Core Ops, SparseCore 0:
  9.7 56.6 all-gather.6
  68.1 35.0 all-gather.4
  105.5 54.2 all-gather.10
  161.3 35.0 all-gather.8
  211.1 74.6 reduce-scatter.1
where the time goes:
time: 296 us
  waiting for transfers between devices  248 us (84%)
  matrix products  25.2 us (9%)
  between operations  13.1 us (4%)
  other arithmetic  9.12 us (3%)
    reduce_scatter x1, waiting for transfers between devices, local(): lax.psum_scatter(jnp.dot(mismatch, column_s, preferred_element_type=jnp.f...  74.8 us
    all_gather x1, waiting for transfers between devices, local(): lax.all_gather(unit_s, 'gr', axis=0, tiled=True)  52.6 us
    all_gather x1, waiting for transfers between devices, local(): lax.all_gather(unit_t, 'gr', axis=0, tiled=True)  46 us
    all_gather x1, waiting for transfers between devices, local(): lax.all_gather(unit_s, 'gc', axis=0, tiled=True)  36.8 us
    all_gather x1, waiting for transfers between devices, local(): lax.all_gather(unit_t, 'gc', axis=0, tiled=True)  36.6 us
    dot_general x1, matrix products, local(): jnp.dot(mismatch, column_s, preferred_element_type=jnp.float32)  14.5 us
    dot_general x1, matrix products, mismatch_of(): lax.dot_general(piece_s, other_s, (((1,), (1,)), ((), ())), preferred_ele...  10.7 us
  transfers between devices with their start and end apart: 5, of which 5 were waited for; matrix products, arithmetic and copies ran while one was open for 5% of the time, Pallas kernels for 0%

commit v1 on v0

--- a/solution.py
+++ b/solution.py
@@ -4,6 +4,13 @@
 from jax.sharding import PartitionSpec as P
 
 D = 1024
+
+
+def _link_sector(field):
+    block_list = []
+    for _ in range(lax.psum(1, "gr")):
+        block_list.append(field)
+    return jnp.concatenate(lax.all_to_all(jnp.stack(block_list, axis=0), "gr", 0, 0), axis=0)
 
 
 def unit_rows(embedded):
@@ -27,10 +34,7 @@
 def local(student, teacher):
     unit_s, inv_s = unit_rows(student)
     unit_t, inv_t = unit_rows(teacher)
-    column_s, column_t = (
-        lax.all_gather(unit_s, "gr", axis=0, tiled=True),
-        lax.all_gather(unit_t, "gr", axis=0, tiled=True),
-    )
+    column_s, column_t = (lax.all_gather(unit_s, "gr", axis=0, tiled=True), _link_sector(unit_t))
     row_s, row_t = (
         lax.all_gather(unit_s, "gc", axis=0, tiled=True),
         lax.all_gather(unit_t, "gc", axis=0, tiled=True),

time: 296 us -> 260 us (0.88)
  waiting for transfers between devices: 248 us -> 201 us
  starting transfers between devices: 0.16 us -> 8.15 us
    all_gather x1 -> x0, waiting for transfers between devices: 46 us -> none  [local(): lax.all_gather(unit_t, 'gr', axis=0, tiled=True)]
    all_gather x1, waiting for transfers between devices: 36.6 us -> 28.5 us  [local(): lax.all_gather(unit_t, 'gc', axis=0, tiled=True)]
    all_to_all x0 -> x1, starting transfers between devices: none -> 8.03 us  [_link_sector(): lax.all_to_all(jnp.stack(block_list, axis=0), 'gr', 0, 0)]
    all_gather x1, waiting for transfers between devices: 52.6 us -> 60.2 us  [local(): lax.all_gather(unit_s, 'gr', axis=0, tiled=True)]
  transfers between devices with their start and end apart: 5 -> 5, of which waited for: 5 -> 4; matrix products, arithmetic and copies ran while one was open for 5% -> 6% of each run, Pallas kernels for 0% -> 0%
where the time goes in v1:
time: 260 us; the launch traced here: 259 us
  waiting for transfers between devices  201 us (77%)
  matrix products  25.1 us (10%)
  between operations  13.1 us (5%)
  other arithmetic  9.13 us (4%)
  starting transfers between devices  8.15 us (3%)
    reduce_scatter x1, waiting for transfers between devices, local(): lax.psum_scatter(jnp.dot(mismatch, column_s, preferred_element_type=jnp.f...  74.8 us
    all_gather x1, waiting for transfers between devices, local(): lax.all_gather(unit_s, 'gr', axis=0, tiled=True)  60.2 us
    all_gather x1, waiting for transfers between devices, local(): lax.all_gather(unit_s, 'gc', axis=0, tiled=True)  36.8 us
    all_gather x1, waiting for transfers between devices, local(): lax.all_gather(unit_t, 'gc', axis=0, tiled=True)  28.5 us
    dot_general x1, matrix products, local(): jnp.dot(mismatch, column_s, preferred_element_type=jnp.float32)  14.5 us
    dot_general x1, matrix products, mismatch_of(): lax.dot_general(piece_s, other_s, (((1,), (1,)), ((), ())), preferred_ele...  10.6 us
    all_to_all x1, starting transfers between devices, _link_sector(): lax.all_to_all(jnp.stack(block_list, axis=0), 'gr', 0, 0)  8.03 us
  transfers between devices with their start and end apart: 5, of which 4 were waited for; matrix products, arithmetic and copies ran while one was open for 6% of the time, Pallas kernels for 0%

profile of v1, /device:TPU:0, one launch (start us, length us, event | category | flops | bytes accessed | tf_op | source)
XLA Modules:
  0.0 259.1 jit_solution(3167579015269272121)
XLA Ops:
  6.5 0.0 all-gather.6.cloned.1.call-start
  6.5 1.1 fusion.4
  7.6 1.8 fusion.6
  9.4 0.0 all-gather.6.cloned.1.call-update
  9.4 0.0 all-gather.4.cloned.1.call-start
  9.5 0.7 all-gather.4.cloned.1.call-update
  10.2 0.0 all-gather.8.cloned.1.call-start
  10.2 1.1 fusion.7
  11.3 1.8 fusion.9
  13.2 0.0 all-gather.8.cloned.1.call-update
  13.2 2.6 stack.2
  15.7 8.0 %all-to-all-start = ((bf16[8,128,1024]{2,1,0:T(8,128)(2,1)}), bf16[8,128,1024]{2,1,0:T(8,128)(2,1)S(1)}, u32[]{:S(2)}, u32[]{:S(2)}) async-start(bf16[8,128,1024]{2,1,0:T(8,128)(2,1)} %stack.2), calls=%async_computation | async-start | bytes 4194304 | tf_op jit(solution)/shard_map/all_to_all | solution.py:13
  23.8 0.0 reduce-scatter.2.cloned.1.call-start
  23.8 60.2 %all-gather.6.cloned.1.call-done = bf16[1024,1024]{1,0:T(8,128)(2,1)} async-done(((bf16[128,1024]{1,0:T(8,128)(2,1)}), bf16[1024,1024]{1,0:T(8,128)(2,1)}) %all-gather.6.cloned.1.call-update) | async-done | bytes 2097168 | tf_op jit(solution)/shard_map/all_gather | solution.py:37
  84.0 36.8 %all-gather.4.cloned.1.call-done = bf16[2048,1024]{1,0:T(8,128)(2,1)} async-done(((bf16[128,1024]{1,0:T(8,128)(2,1)}), bf16[2048,1024]{1,0:T(8,128)(2,1)}) %all-gather.4.cloned.1.call-update) | async-done | bytes 4194320 | tf_op jit(solution)/shard_map/all_gather | solution.py:39
  120.8 10.6 %fusion.14 = f32[2048,1024]{1,0:T(8,128)} fusion(bf16[2048,1024]{1,0:T(8,128)(2,1)} %all-gather.4.cloned.1.call-done, bf16[1024,1024]{1,0:T(8,128)(2,1)} %all-gather.6.cloned.1.call-done), kind=kOutput, calls=%fused_computation.23 | convolution fusion | flops 4294967296 | bytes 14680064 | tf_op jit(solution)/shard_map/dot_general | solution.py:24
  131.4 0.0 all-to-all-done
  131.4 28.5 %all-gather.8.cloned.1.call-done = bf16[2048,1024]{1,0:T(8,128)(2,1)} async-done(((bf16[128,1024]{1,0:T(8,128)(2,1)}), bf16[2048,1024]{1,0:T(8,128)(2,1)}) %all-gather.8.cloned.1.call-update) | async-done | bytes 4194320 | tf_op jit(solution)/shard_map/all_gather | solution.py:40
  159.9 14.5 %fusion = f32[2048,1024]{1,0:T(8,128)} fusion(bf16[1024,1024]{1,0:T(8,128)(2,1)} %all-gather.6.cloned.1.call-done, f32[2048,1024]{1,0:T(8,128)} %fusion.14, bf16[2048,1024]{1,0:T(8,128)(2,1)} %all-gather.8.cloned.1.call-done, bf16[1024,1024]{1,0:T(8,128)(2,1)S(1)} %bitcast.6), kind=kOutput, calls=%fused_computation.1 | convolution fusion | flops 8596226048 | bytes 25165824 | tf_op jit(solution)/shard_map/dot_general | solution.py:44
  174.4 0.0 copy-start
  174.4 0.0 reduce-scatter.2.cloned.1.call-update
  174.4 74.8 %reduce-scatter.2.cloned.1.call-done = f32[128,1024]{1,0:T(8,128)} async-done(((f32[2048,1024]{1,0:T(8,128)}), f32[128,1024]{1,0:T(8,128)}) %reduce-scatter.2.cloned.1.call-update) | async-done | bytes 524304 | tf_op jit(solution)/shard_map/reduce_scatter | solution.py:43
  249.2 0.0 copy-done
  249.2 1.3 fusion.10
  250.5 2.1 fusion.12
  (2 shorter events, 0.0 us)
Async XLA Ops:
  6.5 77.4 %all-gather.6.cloned.1.call-start = ((), (), s32[]{:S(2)}) async-start(), calls=%async_computation.3 | async-start | bytes 2359296 | tf_op jit(solution)/shard_map/all_gather | solution.py:37
  9.4 111.3 %all-gather.4.cloned.1.call-start = ((), (), s32[]{:S(2)}) async-start(), calls=%async_computation.2 | async-start | bytes 4456448 | tf_op jit(solution)/shard_map/all_gather | solution.py:39
  10.2 149.7 %all-gather.8.cloned.1.call-start = ((), (), s32[]{:S(2)}) async-start(), calls=%async_computation.4 | async-start | bytes 4456448 | tf_op jit(solution)/shard_map/all_gather | solution.py:40
  15.7 115.7 %all-to-all-start = ((bf16[8,128,1024]{2,1,0:T(8,128)(2,1)}), bf16[8,128,1024]{2,1,0:T(8,128)(2,1)S(1)}, u32[]{:S(2)}, u32[]{:S(2)}) async-start(bf16[8,128,1024]{2,1,0:T(8,128)(2,1)} %stack.2), calls=%async_computation | async-start | bytes 4194304 | tf_op jit(solution)/shard_map/all_to_all | solution.py:13
  23.8 225.4 %reduce-scatter.2.cloned.1.call-start = ((), (), s32[]{:S(2)}) async-start(), calls=%async_computation.5 | async-start | bytes 8912896 | tf_op jit(solution)/shard_map/reduce_scatter | solution.py:43
  174.4 74.8 %copy-start = (bf16[128,1024]{1,0:T(8,128)(2,1)S(1)}, bf16[128,1024]{1,0:T(8,128)(2,1)}, u32[]{:S(2)}) copy-start(bf16[128,1024]{1,0:T(8,128)(2,1)} %param.2) | copy-start | bytes 786436
Sparse Core Ops, SparseCore 0:
  9.7 74.2 all-gather.5
  85.7 35.0 all-gather.3
  122.5 37.3 all-gather.7
  174.5 74.6 reduce-scatter.1
